TPU v7x, 32 devices: a whole 2x2x4 slice. The times are simulated.
32 devices in a mesh: group: 2 (over x), space: 16 (over z, y, core).
Axes of the slice: x: 2, y: 2, z: 4, core: 2. Of those that a mesh axis runs over, the one named last changes fastest.
Arguments:
- states: float32 [4, 69, 384, 128], P('group', None, 'space'), parts along dimension 0, may hold values from -6 to 6
- plan: int32 [4], P('group'), parts along dimension 0, may hold values from 0 to 1, each once
- member_ids: int32 [4], P('group'), parts along dimension 0, may hold values from 0 to 15
- member_table: float32 [16, 512], replicated, may hold values from -6 to 6
- enc_weight: bfloat16 [3, 3, 69, 512], replicated, may hold values from -0.25 to 0.25
- proc_weight: bfloat16 [2, 3, 3, 512, 512], replicated, may hold values from -0.09375 to 0.09375
- dec_weight: bfloat16 [3, 3, 512, 69], replicated, may hold values from -0.1875 to 0.1875
Outputs:
- forecasts: float32 [2, 4, 69, 384, 128], P(None, 'group', None, 'space'), parts along dimension 1
There are 2 independent parts, one for each index of `group`. A program takes and returns all parts, laid end to end along the dimension named above; an argument that names none is the same for every part. Nothing has to cross between parts.
Inputs may be any that keep to these rules, and one draw needn't show every extreme that they name: plan is a permutation of the 2 member slots. member_ids index rows of member_table.
All inputs are finite; a program needn't handle non-finite values.
Results may differ from a plain program's by a relative error of at most 0.012.
Values may be sent and summed in bfloat16 or wider, within the bound.
No kernel may reach another device: no remote copies, remote signals or barrier semaphores. Data moves between devices by JAX's collectives and lax.ppermute only.
A program may use at most 128 MiB of HBM per device.

v0:
```python
import functools

import jax
import jax.numpy as jnp
from jax import lax
from jax.experimental import pallas as pl
from jax.experimental.pallas import tpu as pltpu
from jax.sharding import PartitionSpec as P

STEPS = 2
VPAD = 80
WEST = 7
EAST = 8
EDGE = 8
KENC = 256
F32 = jnp.float32
BF16 = jnp.bfloat16


def chunks(total, size):
    count = max(1, total // size)
    base, extra = divmod(total, count)
    start, out = 0, []
    for k in range(count):
        n = base + (1 if k < extra else 0)
        out.append((start, n))
        start += n
    return out


def gelu(x):
    inner = x * (0.7978845608028654 + 0.035677408136300125 * (x * x))
    half = 0.5 * x
    return half + half * jnp.tanh(inner)


def nt_dot(lhs, rhs):
    return lax.dot_general(lhs, rhs, (((1,), (1,)), ((), ())), preferred_element_type=F32)


def dot(lhs, rhs):
    return jnp.dot(lhs, rhs, preferred_element_type=F32)


def step_kernel(step, dims, *refs):
    members, nvars, cols, lat, hid = dims
    half = lat // 2
    coarse = cols // 2
    first, last = step == 0, step == STEPS - 1
    refs = list(refs)
    plan_ref, ids_ref, field_hbm, west, east = refs[:5]
    table_ref, wenc_hbm, wproc_hbm, wdec_hbm = refs[5:9]
    refs = refs[9 if first else 10 :]
    out_hbm = refs[0]
    refs = refs[1:]
    if not last:
        wedge_ref, eedge_ref = refs[:2]
        refs = refs[2:]
    (flds, wenc_ref, wproc, wdec_ref, halo) = refs[:5]
    (tmp, xe, xo, x1, x2, h0, h1, oo, sems, wsems) = refs[5:]

    def load_field(member):
        source = field_hbm.at[plan_ref[member]] if first else out_hbm.at[step - 1, member]
        return pltpu.make_async_copy(source, flds.at[member], sems.at[member])

    def save_field(member):
        return pltpu.make_async_copy(
            flds.at[member], out_hbm.at[step, member], sems.at[members + member]
        )

    load_enc = pltpu.make_async_copy(wenc_hbm, wenc_ref.at[:, 0 : 3 * VPAD], wsems.at[2])
    load_dec = pltpu.make_async_copy(wdec_hbm, wdec_ref, wsems.at[3])
    load_w = [
        [
            pltpu.make_async_copy(
                wproc_hbm.at[layer, a], wproc.at[layer, a], wsems.at[4 + 3 * layer + a]
            )
            for a in range(3)
        ]
        for layer in range(2)
    ]
    load_field(0).start()
    pick = (
        lax.broadcasted_iota(jnp.int32, (half, lat), 1)
        == 2 * lax.broadcasted_iota(jnp.int32, (half, lat), 0) + 1
    ).astype(F32).astype(BF16)
    lane = lax.broadcasted_iota(jnp.int32, (VPAD, lat), 1)
    tmp[...] = jnp.zeros(tmp.shape, F32)
    wenc_ref[:, 3 * VPAD :] = jnp.zeros((3, KENC - 3 * VPAD, hid), BF16)

    def take_in(index, values):
        buf = index % tmp.shape[0]
        tmp[buf, 0:nvars, :] = values
        values = tmp[buf]
        one = pltpu.roll(values, 1, 1)
        two = jnp.where(lane < 2, 0.0, pltpu.roll(values, 2, 1))
        stacked = jnp.concatenate(
            [two, one, values, jnp.zeros((KENC - 3 * VPAD, lat), F32)], axis=0
        ).astype(BF16)
        picked = nt_dot(pick, stacked).astype(BF16)
        target = xe if index % 2 == 0 else xo
        target[(index // 2) * half : (index // 2 + 1) * half, :] = picked

    def spread(values, ncols, start, dilation, target):
        rows = lax.broadcasted_iota(jnp.int32, (ncols * half, hid), 0) & (half - 1)
        down = jnp.where(rows < dilation, 0.0, pltpu.roll(values, dilation, 0))
        up = jnp.where(
            rows >= half - dilation, 0.0, pltpu.roll(values, ncols * half - dilation, 0)
        )
        where = slice(start * half, (start + ncols) * half)
        target[where, 0:hid] = down.astype(BF16)
        target[where, hid : 2 * hid] = values.astype(BF16)
        target[where, 2 * hid : 3 * hid] = up.astype(BF16)

    always = plan_ref[0] >= 0

    def alone(items):
        return [piece for _, piece in items]

    def evenly(items):
        return [((k + 0.5) / len(items), piece) for k, piece in enumerate(items)]

    def block(items):
        if not isinstance(items[0], tuple):
            items = evenly(items)

        @pl.when(always)
        def _():
            for _, piece in sorted(items, key=lambda item: item[0]):
                piece()

    def slot_of(member):
        return plan_ref[member] if first else member

    def open_halo(member):
        halo[0] = west[slot_of(member)].astype(F32)
        halo[1] = east[slot_of(member)].astype(F32)

    def intake(member):
        fld = flds.at[member]

        def own(p):
            take_in(WEST + p, fld[pl.ds(p, nvars, stride=cols), :])

        def from_west(p):
            take_in(p, halo[0, pl.ds(EDGE - WEST + p, nvars, stride=EDGE), :])

        def from_east(p):
            take_in(WEST + cols + p, halo[1, pl.ds(p, nvars, stride=EDGE), :])

        return (
            [functools.partial(from_west, p) for p in range(WEST)]
            + [functools.partial(own, p) for p in range(cols)]
            + [functools.partial(from_east, p) for p in range(EAST)]
        )

    def encode(member):
        def piece(start, n):
            mvec = table_ref[pl.ds(ids_ref[plan_ref[member]], 1), :]
            rows = slice(start * half, (start + n) * half)
            after = slice((start + 1) * half, (start + 1 + n) * half)
            hidden = dot(xe[rows, :], wenc_ref[0]) + dot(xo[rows, :], wenc_ref[1])
            hidden = hidden + dot(xe[after, :], wenc_ref[2]) + mvec
            lo, hi = max(start, 1), min(start + n, coarse + 6)
            h0[(lo - 1) * half : (hi - 1) * half, :] = hidden[
                (lo - start) * half : (hi - start) * half
            ]
            spread(gelu(hidden), n, start, 1, x1)

        return [(c, functools.partial(piece, *c)) for c in chunks(coarse + 7, 4)]

    def layer0():
        def piece(start, n):
            hidden = h0[start * half : (start + n) * half, :]
            for a in range(3):
                rows = slice((start + a) * half, (start + a + n) * half)
                hidden = hidden + dot(x1[rows, :], wproc[0, a])
            lo, hi = max(start, 2), min(start + n, coarse + 3)
            h1[(lo - 2) * half : (hi - 2) * half, :] = hidden[
                (lo - start) * half : (hi - start) * half
            ]
            spread(gelu(hidden), n, start, 2, x2)

        return [(c, functools.partial(piece, *c)) for c in chunks(coarse + 5, 4)]

    def layer1():
        def piece(start, n):
            hidden = h1[start * half : (start + n) * half, :]
            for a in range(3):
                rows = slice((start + 2 * a) * half, (start + 2 * a + n) * half)
                hidden = hidden + dot(x2[rows, :], wproc[1, a])
            outgoing = gelu(hidden)
            rows = lax.broadcasted_iota(jnp.int32, (n * half, hid), 0) & (half - 1)
            up = jnp.where(rows >= half - 1, 0.0, pltpu.roll(outgoing, n * half - 1, 0))
            where = slice(start * half, (start + n) * half)
            oo[where, 0:hid] = outgoing.astype(BF16)
            oo[where, hid : 2 * hid] = up.astype(BF16)

        return [(c, functools.partial(piece, *c)) for c in chunks(coarse + 1, 4)]

    def decode(member):
        fld = flds.at[member]

        def piece(start, n):
            key = lax.broadcasted_iota(jnp.int32, (2 * lat, 2 * lat), 0)
            spot = (key // half % 2) * lat + 2 * (key % half) + key // lat
            weave = lax.broadcasted_iota(jnp.int32, (2 * lat, 2 * lat), 1) == spot
            weave = weave.astype(F32).astype(BF16)
            v = VPAD
            here = slice(start * half, (start + n) * half)
            nxt = slice((start + 1) * half, (start + 1 + n) * half)
            tap = [wdec_ref[k * v : (k + 1) * v] for k in range(9)]
            g1 = nt_dot(jnp.concatenate([tap[4], tap[5], tap[7], tap[8]]), oo[here, 0:hid])
            g2 = nt_dot(jnp.concatenate([tap[3], tap[6]]), oo[here, hid : 2 * hid])
            g3 = nt_dot(jnp.concatenate([tap[1], tap[2]]), oo[nxt, 0:hid])
            g4 = nt_dot(tap[0], oo[nxt, hid : 2 * hid])
            parts = (
                (g1[0:v], g1[v : 2 * v] + g2[0:v]),
                (
                    g1[2 * v : 3 * v] + g3[0:v],
                    g1[3 * v : 4 * v] + g2[v : 2 * v] + g3[v : 2 * v] + g4,
                ),
            )
            for pair in range(n // 2):
                lanes = slice(pair * lat, (pair + 1) * lat)
                for lon_parity in range(2):
                    even, odd = parts[lon_parity]
                    both = jnp.concatenate([even[:, lanes], odd[:, lanes]], axis=1)
                    woven = dot(both.astype(BF16), weave)
                    for side in range(2):
                        p = 2 * (start + 2 * pair + side) + lon_parity
                        update = woven[:, side * lat : (side + 1) * lat]
                        there = pl.ds(p, nvars, stride=cols)
                        fld[there, :] = fld[there, :] + update[0:nvars]

        spans = [(2 * start, 2 * n) for start, n in chunks(coarse // 2, 2)]
        return [(c, functools.partial(piece, *c)) for c in spans]

    def close(member):
        save_field(member).start()
        if not last:
            fld = flds.at[member]
            for edge_ref, start in ((wedge_ref, 0), (eedge_ref, cols - EDGE)):
                rows = [fld[v * cols + start : v * cols + start + EDGE, :] for v in range(nvars)]
                edge_ref[member] = jnp.concatenate(rows, axis=0).astype(BF16)

    def roll_out(member, carry):
        load_field(member).wait()

        @pl.when(member == 0)
        def weights():
            load_enc.start()
            for load in load_w[0]:
                load.start()
            for other in range(1, members):
                load_field(other).start()

        open_halo(member)
        block(intake(member))

        @pl.when(member == 0)
        def encoder_weight():
            load_enc.wait()

        block(alone(encode(member)))

        @pl.when(member == 0)
        def layer0_weight():
            for load in load_w[0]:
                load.wait()
            for load in load_w[1]:
                load.start()
            load_dec.start()

        block(alone(layer0()))

        @pl.when(member == 0)
        def layer1_weight():
            for load in load_w[1]:
                load.wait()
            load_dec.wait()

        block(alone(layer1()))
        block(alone(decode(member)))
        close(member)
        return carry

    lax.fori_loop(0, members, roll_out, 0)
    for member in range(members):
        save_field(member).wait()


def run_step(step, dims, plan, ids, field, west, east, table, wenc, wproc, wdec, buf):
    members, nvars, cols, lat, hid = dims
    half, coarse = lat // 2, cols // 2
    smem = pl.BlockSpec(memory_space=pltpu.SMEM)
    hbm = pl.BlockSpec(memory_space=pl.ANY)
    vmem = pl.BlockSpec(memory_space=pltpu.VMEM)
    args = [plan, ids, field, west, east, table, wenc, wproc, wdec]
    in_specs = [smem, smem, hbm, vmem, vmem, vmem, hbm, hbm, hbm]
    aliases = {}
    if buf is not None:
        aliases = {len(args): 0}
        args.append(buf)
        in_specs.append(hbm)
    out_shape = [jax.ShapeDtypeStruct((STEPS, members, nvars * cols, lat), F32)]
    out_specs = [hbm]
    if step < STEPS - 1:
        out_shape += [jax.ShapeDtypeStruct((members, nvars * EDGE, lat), BF16)] * 2
        out_specs += [vmem] * 2
    scratch = [
        pltpu.VMEM((members, nvars * cols, lat), F32),
        pltpu.VMEM((3, KENC, hid), BF16),
        pltpu.VMEM(wproc.shape, BF16),
        pltpu.VMEM(wdec.shape, BF16),
        pltpu.VMEM((2, nvars * EDGE, lat), F32),
        pltpu.VMEM((8, VPAD, lat), F32),
        pltpu.VMEM(((coarse + 8) * half, KENC), BF16),
        pltpu.VMEM(((coarse + 7) * half, KENC), BF16),
        pltpu.VMEM(((coarse + 7) * half, 3 * hid), BF16),
        pltpu.VMEM(((coarse + 5) * half, 3 * hid), BF16),
        pltpu.VMEM(((coarse + 5) * half, hid), F32),
        pltpu.VMEM(((coarse + 1) * half, hid), F32),
        pltpu.VMEM(((coarse + 1) * half, 2 * hid), BF16),
        pltpu.SemaphoreType.DMA((2 * members,)),
        pltpu.SemaphoreType.DMA((10,)),
    ]
    flops = members * 2 * half * hid * hid * 9 * (2 * coarse + 6)
    return pl.pallas_call(
        functools.partial(step_kernel, step, dims),
        out_shape=out_shape,
        in_specs=in_specs,
        out_specs=out_specs,
        scratch_shapes=scratch,
        input_output_aliases=aliases,
        cost_estimate=pl.CostEstimate(flops=flops, bytes_accessed=16 * 2**20, transcendentals=0),
        compiler_params=pltpu.CompilerParams(vmem_limit_bytes=44 * 2**20),
        name="rollout_step%d" % step,
    )(*args)


def exchange(last, first):
    count = lax.axis_size("space")
    forward = [(i, (i + 1) % count) for i in range(count)]
    backward = [(target, source) for source, target in forward]
    return lax.ppermute(last, "space", forward), lax.ppermute(first, "space", backward)


def local(states, plan, member_ids, member_table, enc_weight, proc_weight, dec_weight):
    members, nvars, cols, lat = states.shape
    hid = proc_weight.shape[-1]
    dims = (members, nvars, cols, lat, hid)

    pad_v = ((0, 0), (0, 0), (0, VPAD - nvars), (0, 0))
    wenc = jnp.pad(enc_weight, pad_v).reshape(3, 3 * VPAD, hid)
    wdec = jnp.pad(jnp.swapaxes(dec_weight, 2, 3), pad_v).reshape(9 * VPAD, hid)
    wproc = proc_weight.reshape(proc_weight.shape[0], 3, 3 * hid, hid)

    flat_edge = (members, nvars * EDGE, lat)
    west, east = exchange(
        states[:, :, cols - EDGE :].astype(BF16).reshape(flat_edge),
        states[:, :, :EDGE].astype(BF16).reshape(flat_edge),
    )
    flat = states.reshape(members, nvars * cols, lat)
    buf = None
    for step in range(STEPS):
        result = run_step(
            step, dims, plan, member_ids, flat, west, east, member_table, wenc, wproc, wdec, buf
        )
        buf = result[0]
        if step < STEPS - 1:
            west, east = exchange(result[2], result[1])
    return buf.reshape(STEPS, members, nvars, cols, lat)


def solution(mesh):
    return jax.shard_map(
        local,
        mesh=mesh,
        in_specs=(P("group", None, "space", None), P("group"), P("group"), P(), P(), P(), P()),
        out_specs=P(None, "group", None, "space", None),
        check_vma=False,
    )
```

profile of v0, /device:TPU:0, one launch (start us, length us, event | category | flops | bytes accessed | tf_op | source)
XLA Modules:
  0.0 95.2 jit_solution(14883667377265518664)
XLA Ops:
  0.0 0.0 copy-start
  0.0 0.0 copy-start.4
  0.0 0.0 copy-start.5
  0.0 0.0 copy-start.2
  0.0 1.7 %convert.4 = bf16[2,69,24,128]{3,2,1,0:T(8,128)(2,1)S(1)} convert(f32[2,69,24,128]{3,2,1,0:T(8,128)} %param.7) | non-fusion elementwise | flops 423936 | bytes 2543616 | tf_op jit(solution)/shard_map/convert.1
  1.7 0.1 slice_bitcast_fusion
  1.8 5.5 %collective-permute-start.1 = (bf16[2,552,128]{2,1,0:T(8,128)(2,1)S(1)}, bf16[2,552,128]{2,1,0:T(8,128)(2,1)S(1)}, u32[]{:S(2)}, u32[]{:S(2)}) collective-permute-start(bf16[2,552,128]{2,1,0:T(8,128)(2,1)S(1)} %get-tuple-element.11), channel_id=1, source_target_pairs={{1,0},{2,1},{3,2},{4,3},{5,4},{6,5},{7,6},{8,7},{9,8},{10,9},{11,1... | collective-permute-start | bytes 847880 | tf_op jit(solution)/shard_map/ppermute | solution.py:346
  7.4 0.0 collective-permute-start
  7.4 0.0 copy-done.4
  7.4 0.1 pad.7
  7.4 0.0 copy-done.5
  7.4 0.1 pad.8
  7.5 4.0 %collective-permute-done.1.refs_4_ = bf16[2,552,128]{2,1,0:T(8,128)(2,1)S(1)} collective-permute-done((bf16[2,552,128]{2,1,0:T(8,128)(2,1)S(1)}, bf16[2,552,128]{2,1,0:T(8,128)(2,1)S(1)}, u32[]{:S(2)}, u32[]{:S(2)}) %collective-permute-start.1) | collective-permute-done | bytes 282656 | tf_op jit(solution)/shard_map/ppermute | solution.py:346
  11.5 4.6 %collective-permute-done.refs_3_ = bf16[2,552,128]{2,1,0:T(8,128)(2,1)S(1)} collective-permute-done((bf16[2,552,128]{2,1,0:T(8,128)(2,1)S(1)}, bf16[2,552,128]{2,1,0:T(8,128)(2,1)S(1)}, u32[]{:S(2)}, u32[]{:S(2)}) %collective-permute-start) | collective-permute-done | bytes 282656 | tf_op jit(solution)/shard_map/ppermute | solution.py:346
  16.1 0.0 copy-done
  16.1 0.0 copy-done.1
  16.1 0.0 copy-done.3
  16.1 0.0 copy-done.2
  16.1 34.7 %rollout_step0.1 = (f32[2,2,1656,128]{3,2,1,0:T(8,128)}, bf16[2,552,128]{2,1,0:T(8,128)(2,1)S(1)}, bf16[2,552,128]{2,1,0:T(8,128)(2,1)S(1)}) custom-call(s32[2]{0:T(128)S(1)} %copy-done.2, s32[2]{0:T(128)S(1)} %copy-done.3, f32[2,1656,128]{2,1,0:T(8,128)S(1)} %bitcast.10, bf16[2,552,128]{2,1,0:T(8,128)(2,1)S(1)} %collective-permute-done.refs_3_, ...), custom_call_target="tpu_custom_call" | custom-call | flops 18119393280 | bytes 16777216 | tf_op jit(solution)/shard_map/rollout_step0/pallas_call | solution.py:329
  50.8 0.1 collective-permute-start.2
  50.8 4.4 %collective-permute-start.3 = (bf16[2,552,128]{2,1,0:T(8,128)(2,1)S(1)}, bf16[2,552,128]{2,1,0:T(8,128)(2,1)S(1)}, u32[]{:S(2)}, u32[]{:S(2)}) collective-permute-start(bf16[2,552,128]{2,1,0:T(8,128)(2,1)S(1)} %get-tuple-element.9), channel_id=1, source_target_pairs={{1,0},{2,1},{3,2},{4,3},{5,4},{6,5},{7,6},{8,7},{9,8},{10,9},{11,1... | collective-permute-start | bytes 847880 | tf_op jit(solution)/shard_map/ppermute | solution.py:346
  55.3 4.3 %collective-permute-done.2.refs_3_ = bf16[2,552,128]{2,1,0:T(8,128)(2,1)S(1)} collective-permute-done((bf16[2,552,128]{2,1,0:T(8,128)(2,1)S(1)}, bf16[2,552,128]{2,1,0:T(8,128)(2,1)S(1)}, u32[]{:S(2)}, u32[]{:S(2)}) %collective-permute-start.2) | collective-permute-done | bytes 282656 | tf_op jit(solution)/shard_map/ppermute | solution.py:346
  59.5 0.0 collective-permute-done.3.refs_4_
  59.5 35.5 %rollout_step1.1 = f32[2,2,1656,128]{3,2,1,0:T(8,128)} custom-call(s32[2]{0:T(128)S(1)} %copy-done.2, s32[2]{0:T(128)S(1)} %copy-done.3, f32[2,1656,128]{2,1,0:T(8,128)S(1)} %bitcast.11, bf16[2,552,128]{2,1,0:T(8,128)(2,1)S(1)} %collective-permute-done.2.refs_3_, ...), custom_call_target="tpu_custom_call", output_to_operand_aliasing={{}: (9, {})} | custom-call | flops 18119393280 | bytes 16777216 | tf_op jit(solution)/shard_map/rollout_step1/pallas_call | solution.py:329
  (2 shorter events, 0.0 us)
Async XLA Ops:
  0.0 16.1 %copy-start = (f32[2,69,24,128]{3,2,1,0:T(8,128)S(1)}, f32[2,69,24,128]{3,2,1,0:T(8,128)}, u32[]{:S(2)}) copy-start(f32[2,69,24,128]{3,2,1,0:T(8,128)} %param.7) | copy-start | bytes 5087236
  0.0 7.4 %copy-start.4 = (bf16[3,3,69,512]{3,2,1,0:T(8,128)(2,1)S(1)}, bf16[3,3,69,512]{3,2,1,0:T(8,128)(2,1)}, u32[]{:S(2)}) copy-start(bf16[3,3,69,512]{3,2,1,0:T(8,128)(2,1)} %param.11) | copy-start | bytes 1907716
  0.0 7.4 %copy-start.5 = (bf16[3,3,512,69]{2,3,1,0:T(8,128)(2,1)S(1)}, bf16[3,3,512,69]{2,3,1,0:T(8,128)(2,1)}, u32[]{:S(2)}) copy-start(bf16[3,3,512,69]{2,3,1,0:T(8,128)(2,1)} %param.13) | copy-start | bytes 1907716
  0.0 16.1 %copy-start.1 = (f32[16,512]{1,0:T(8,128)S(1)}, f32[16,512]{1,0:T(8,128)}, u32[]{:S(2)}) copy-start(f32[16,512]{1,0:T(8,128)} %refs_5_.3) | copy-start | bytes 98308
  0.0 16.1 %copy-start.3 = (s32[2]{0:T(128)S(1)}, s32[2]{0:T(128)}, u32[]{:S(2)}) copy-start(s32[2]{0:T(128)} %refs_1_.3) | copy-start | bytes 28
  0.0 16.1 %copy-start.2 = (s32[2]{0:T(128)S(1)}, s32[2]{0:T(128)}, u32[]{:S(2)}) copy-start(s32[2]{0:T(128)} %refs_0_.3) | copy-start | bytes 28
  1.8 9.6 %collective-permute-start.1 = (bf16[2,552,128]{2,1,0:T(8,128)(2,1)S(1)}, bf16[2,552,128]{2,1,0:T(8,128)(2,1)S(1)}, u32[]{:S(2)}, u32[]{:S(2)}) collective-permute-start(bf16[2,552,128]{2,1,0:T(8,128)(2,1)S(1)} %get-tuple-element.11), channel_id=1, source_target_pairs={{1,0},{2,1},{3,2},{4,3},{5,4},{6,5},{7,6},{8,7},{9,8},{10,9},{11,1... | collective-permute-start | bytes 847880 | tf_op jit(solution)/shard_map/ppermute | solution.py:346
  7.4 8.7 %collective-permute-start = (bf16[2,552,128]{2,1,0:T(8,128)(2,1)S(1)}, bf16[2,552,128]{2,1,0:T(8,128)(2,1)S(1)}, u32[]{:S(2)}, u32[]{:S(2)}) collective-permute-start(bf16[2,552,128]{2,1,0:T(8,128)(2,1)S(1)} %get-tuple-element.12), channel_id=1, source_target_pairs={{0,1},{1,2},{2,3},{3,4},{4,5},{5,6},{6,7},{7,8},{8,9},{9,10},{10,1... | collective-permute-start | bytes 847880 | tf_op jit(solution)/shard_map/ppermute | solution.py:346
  50.8 8.8 %collective-permute-start.2 = (bf16[2,552,128]{2,1,0:T(8,128)(2,1)S(1)}, bf16[2,552,128]{2,1,0:T(8,128)(2,1)S(1)}, u32[]{:S(2)}, u32[]{:S(2)}) collective-permute-start(bf16[2,552,128]{2,1,0:T(8,128)(2,1)S(1)} %get-tuple-element.8), channel_id=1, source_target_pairs={{0,1},{1,2},{2,3},{3,4},{4,5},{5,6},{6,7},{7,8},{8,9},{9,10},{10,1... | collective-permute-start | bytes 847880 | tf_op jit(solution)/shard_map/ppermute | solution.py:346
  50.8 8.7 %collective-permute-start.3 = (bf16[2,552,128]{2,1,0:T(8,128)(2,1)S(1)}, bf16[2,552,128]{2,1,0:T(8,128)(2,1)S(1)}, u32[]{:S(2)}, u32[]{:S(2)}) collective-permute-start(bf16[2,552,128]{2,1,0:T(8,128)(2,1)S(1)} %get-tuple-element.9), channel_id=1, source_target_pairs={{1,0},{2,1},{3,2},{4,3},{5,4},{6,5},{7,6},{8,7},{9,8},{10,9},{11,1... | collective-permute-start | bytes 847880 | tf_op jit(solution)/shard_map/ppermute | solution.py:346
where the time goes:
time: 95.3 us; the launch traced here: 95.2 us
  Pallas kernels  70.1 us (74%)
  waiting for transfers between devices  12.8 us (13%)
  starting transfers between devices  10 us (10%)
  other arithmetic  1.71 us (2%)
    pallas_call x2, Pallas kernels, run_step(): pl.pallas_call(functools.partial(step_kernel, step, dims), out_shape=out_...  70.1 us
    ppermute x2, starting transfers between devices, exchange(): lax.ppermute(first, 'space', backward)  9.94 us
    ppermute x2, waiting for transfers between devices, exchange(): lax.ppermute(last, 'space', forward)  8.87 us
    ppermute x2, waiting for transfers between devices, exchange(): lax.ppermute(first, 'space', backward)  3.95 us
  transfers between devices with their start and end apart: 4, of which 3 were waited for; matrix products, arithmetic and copies ran while one was open for 0% of the time, Pallas kernels for 0%

commit v1 on v0

--- a/solution.py
+++ b/solution.py
@@ -167,7 +167,7 @@
             ]
             spread(gelu(hidden), n, start, 1, x1)
 
-        return [(c, functools.partial(piece, *c)) for c in chunks(coarse + 7, 4)]
+        return [(c, functools.partial(piece, *c)) for c in chunks(coarse + 7, 3)]
 
     def layer0():
         def piece(start, n):
@@ -181,7 +181,7 @@
             ]
             spread(gelu(hidden), n, start, 2, x2)
 
-        return [(c, functools.partial(piece, *c)) for c in chunks(coarse + 5, 4)]
+        return [(c, functools.partial(piece, *c)) for c in chunks(coarse + 5, 5)]
 
     def layer1():
         def piece(start, n):
@@ -357,10 +357,9 @@
     wproc = proc_weight.reshape(proc_weight.shape[0], 3, 3 * hid, hid)
 
     flat_edge = (members, nvars * EDGE, lat)
-    west, east = exchange(
-        states[:, :, cols - EDGE :].astype(BF16).reshape(flat_edge),
-        states[:, :, :EDGE].astype(BF16).reshape(flat_edge),
-    )
+    ends = (states[:, :, cols - EDGE :], states[:, :, :EDGE])
+    ends = lax.optimization_barrier(ends)
+    west, east = exchange(*(end.astype(BF16).reshape(flat_edge) for end in ends))
     flat = states.reshape(members, nvars * cols, lat)
     buf = None
     for step in range(STEPS):

time: 95.3 us -> 94.6 us (level)
  local copies, waits for them, and re-layouts: 0.25 us -> 3.76 us
  waiting for transfers between devices: 12.8 us -> 10.7 us
  other arithmetic: 1.71 us -> 0 us
    ppermute x2, waiting for transfers between devices: 3.95 us -> 1.78 us  [exchange(): lax.ppermute(first, 'space', backward)]
    another operation x1 -> x0, other arithmetic: 1.71 us -> none
    slice x0 -> x1, local copies, waits for them, and re-layouts: none -> 1.43 us  [local(): ends = (states[:, :, cols - EDGE:], states[:, :, :EDGE])]
    pad x1, local copies, waits for them, and re-layouts: 0.06 us -> 1.16 us  [local(): wdec = jnp.pad(jnp.swapaxes(dec_weight, 2, 3), pad_v).reshape(9 * VPAD, hid)]
    pad x1, local copies, waits for them, and re-layouts: 0.06 us -> 1.15 us  [local(): wenc = jnp.pad(enc_weight, pad_v).reshape(3, 3 * VPAD, hid)]
  transfers between devices with their start and end apart: 4 -> 4, of which waited for: 3 -> 3; matrix products, arithmetic and copies ran while one was open for 0% -> 2% of each run, Pallas kernels for 0% -> 0%
where the time goes in v1:
time: 94.6 us; the launch traced here: 94.4 us
  Pallas kernels  69.6 us (74%)
  waiting for transfers between devices  10.7 us (11%)
  starting transfers between devices  10.2 us (11%)
  local copies, waits for them, and re-layouts  3.76 us (4%)
    pallas_call x2, Pallas kernels, run_step(): pl.pallas_call(functools.partial(step_kernel, step, dims), out_shape=out_...  69.6 us
    ppermute x2, starting transfers between devices, exchange(): lax.ppermute(first, 'space', backward)  9.94 us
    ppermute x2, waiting for transfers between devices, exchange(): lax.ppermute(last, 'space', forward)  8.87 us
  transfers between devices with their start and end apart: 4, of which 3 were waited for; matrix products, arithmetic and copies ran while one was open for 2% of the time, Pallas kernels for 0%

profile of v1, /device:TPU:0, one launch (start us, length us, event | category | flops | bytes accessed | tf_op | source)
XLA Modules:
  0.0 94.4 jit_solution(16086081564867034044)
XLA Ops:
  0.0 0.0 copy-start
  0.0 0.0 copy-start.1
  0.0 0.0 copy-start.3
  0.0 0.0 copy-start.2
  0.0 1.4 %fusion = (bf16[2,69,8,128]{3,2,1,0:T(8,128)(2,1)S(1)}, bf16[2,69,8,128]{3,2,1,0:T(8,128)(2,1)S(1)}) fusion(f32[2,69,24,128]{3,2,1,0:T(8,128)} %param.7), kind=kLoop, calls=%fused_computation.2 | loop fusion | bytes 1130496 | tf_op jit(solution)/shard_map/slice | solution.py:360
  1.4 5.5 %collective-permute-start.1 = (bf16[2,552,128]{2,1,0:T(8,128)(2,1)S(1)}, bf16[2,552,128]{2,1,0:T(8,128)(2,1)S(1)}, u32[]{:S(2)}, u32[]{:S(2)}) collective-permute-start(bf16[2,552,128]{2,1,0:T(8,128)(2,1)S(1)} %bitcast.20), channel_id=1, source_target_pairs={{1,0},{2,1},{3,2},{4,3},{5,4},{6,5},{7,6},{8,7},{9,8},{10,9},{11,1... | collective-permute-start | bytes 847880 | tf_op jit(solution)/shard_map/ppermute | solution.py:346
  7.0 0.0 collective-permute-start
  7.0 1.2 %pad.7 = bf16[3,3,80,512]{3,2,1,0:T(8,128)(2,1)S(1)} pad(bf16[3,3,69,512]{3,2,1,0:T(8,128)(2,1)} %param.11, bf16[]{:T(256)} %constant.2.clone.1), padding=0_0x0_0x0_11x0_0 | pad | bytes 1373186 | tf_op jit(solution)/shard_map/jit(_pad)/pad | solution.py:355
  8.1 1.2 %pad.8 = bf16[3,3,80,512]{3,2,1,0:T(8,128)(2,1)S(1)} pad(bf16[3,3,69,512]{3,2,1,0:T(8,128)(2,1)} %bitcast.18, bf16[]{:T(256)} %constant.2.clone.1), padding=0_0x0_0x0_11x0_0 | pad | bytes 1373186 | tf_op jit(solution)/shard_map/jit(_pad)/pad | solution.py:356
  9.3 1.8 %collective-permute-done.1.refs_4_ = bf16[2,552,128]{2,1,0:T(8,128)(2,1)S(1)} collective-permute-done((bf16[2,552,128]{2,1,0:T(8,128)(2,1)S(1)}, bf16[2,552,128]{2,1,0:T(8,128)(2,1)S(1)}, u32[]{:S(2)}, u32[]{:S(2)}) %collective-permute-start.1) | collective-permute-done | bytes 282656 | tf_op jit(solution)/shard_map/ppermute | solution.py:346
  11.1 4.6 %collective-permute-done.refs_3_ = bf16[2,552,128]{2,1,0:T(8,128)(2,1)S(1)} collective-permute-done((bf16[2,552,128]{2,1,0:T(8,128)(2,1)S(1)}, bf16[2,552,128]{2,1,0:T(8,128)(2,1)S(1)}, u32[]{:S(2)}, u32[]{:S(2)}) %collective-permute-start) | collective-permute-done | bytes 282656 | tf_op jit(solution)/shard_map/ppermute | solution.py:346
  15.7 0.0 copy-done
  15.7 0.0 copy-done.1
  15.7 0.0 copy-done.3
  15.7 0.0 copy-done.2
  15.7 34.4 %rollout_step0.1 = (f32[2,2,1656,128]{3,2,1,0:T(8,128)}, bf16[2,552,128]{2,1,0:T(8,128)(2,1)S(1)}, bf16[2,552,128]{2,1,0:T(8,128)(2,1)S(1)}) custom-call(s32[2]{0:T(128)S(1)} %copy-done.2, s32[2]{0:T(128)S(1)} %copy-done.3, f32[2,1656,128]{2,1,0:T(8,128)S(1)} %bitcast.16, bf16[2,552,128]{2,1,0:T(8,128)(2,1)S(1)} %collective-permute-done.refs_3_, ...), custom_call_target="tpu_custom_call" | custom-call | flops 18119393280 | bytes 16777216 | tf_op jit(solution)/shard_map/rollout_step0/pallas_call | solution.py:329
  50.1 0.2 collective-permute-start.2
  50.3 4.4 %collective-permute-start.3 = (bf16[2,552,128]{2,1,0:T(8,128)(2,1)S(1)}, bf16[2,552,128]{2,1,0:T(8,128)(2,1)S(1)}, u32[]{:S(2)}, u32[]{:S(2)}) collective-permute-start(bf16[2,552,128]{2,1,0:T(8,128)(2,1)S(1)} %get-tuple-element.13), channel_id=1, source_target_pairs={{1,0},{2,1},{3,2},{4,3},{5,4},{6,5},{7,6},{8,7},{9,8},{10,9},{11,1... | collective-permute-start | bytes 847880 | tf_op jit(solution)/shard_map/ppermute | solution.py:346
  54.8 4.3 %collective-permute-done.2.refs_3_ = bf16[2,552,128]{2,1,0:T(8,128)(2,1)S(1)} collective-permute-done((bf16[2,552,128]{2,1,0:T(8,128)(2,1)S(1)}, bf16[2,552,128]{2,1,0:T(8,128)(2,1)S(1)}, u32[]{:S(2)}, u32[]{:S(2)}) %collective-permute-start.2) | collective-permute-done | bytes 282656 | tf_op jit(solution)/shard_map/ppermute | solution.py:346
  59.0 0.0 collective-permute-done.3.refs_4_
  59.0 35.2 %rollout_step1.1 = f32[2,2,1656,128]{3,2,1,0:T(8,128)} custom-call(s32[2]{0:T(128)S(1)} %copy-done.2, s32[2]{0:T(128)S(1)} %copy-done.3, f32[2,1656,128]{2,1,0:T(8,128)S(1)} %bitcast.17, bf16[2,552,128]{2,1,0:T(8,128)(2,1)S(1)} %collective-permute-done.2.refs_3_, ...), custom_call_target="tpu_custom_call", output_to_operand_aliasing={{}: (9, {})} | custom-call | flops 18119393280 | bytes 16777216 | tf_op jit(solution)/shard_map/rollout_step1/pallas_call | solution.py:329
Async XLA Ops:
  0.0 15.7 %copy-start = (f32[2,69,24,128]{3,2,1,0:T(8,128)S(1)}, f32[2,69,24,128]{3,2,1,0:T(8,128)}, u32[]{:S(2)}) copy-start(f32[2,69,24,128]{3,2,1,0:T(8,128)} %param.7) | copy-start | bytes 5087236
  0.0 15.7 %copy-start.1 = (f32[16,512]{1,0:T(8,128)S(1)}, f32[16,512]{1,0:T(8,128)}, u32[]{:S(2)}) copy-start(f32[16,512]{1,0:T(8,128)} %refs_5_.3) | copy-start | bytes 98308
  0.0 15.7 %copy-start.3 = (s32[2]{0:T(128)S(1)}, s32[2]{0:T(128)}, u32[]{:S(2)}) copy-start(s32[2]{0:T(128)} %refs_1_.3) | copy-start | bytes 28
  0.0 15.7 %copy-start.2 = (s32[2]{0:T(128)S(1)}, s32[2]{0:T(128)}, u32[]{:S(2)}) copy-start(s32[2]{0:T(128)} %refs_0_.3) | copy-start | bytes 28
  1.4 9.6 %collective-permute-start.1 = (bf16[2,552,128]{2,1,0:T(8,128)(2,1)S(1)}, bf16[2,552,128]{2,1,0:T(8,128)(2,1)S(1)}, u32[]{:S(2)}, u32[]{:S(2)}) collective-permute-start(bf16[2,552,128]{2,1,0:T(8,128)(2,1)S(1)} %bitcast.20), channel_id=1, source_target_pairs={{1,0},{2,1},{3,2},{4,3},{5,4},{6,5},{7,6},{8,7},{9,8},{10,9},{11,1... | collective-permute-start | bytes 847880 | tf_op jit(solution)/shard_map/ppermute | solution.py:346
  7.0 8.7 %collective-permute-start = (bf16[2,552,128]{2,1,0:T(8,128)(2,1)S(1)}, bf16[2,552,128]{2,1,0:T(8,128)(2,1)S(1)}, u32[]{:S(2)}, u32[]{:S(2)}) collective-permute-start(bf16[2,552,128]{2,1,0:T(8,128)(2,1)S(1)} %bitcast.19), channel_id=1, source_target_pairs={{0,1},{1,2},{2,3},{3,4},{4,5},{5,6},{6,7},{7,8},{8,9},{9,10},{10,1... | collective-permute-start | bytes 847880 | tf_op jit(solution)/shard_map/ppermute | solution.py:346
  50.1 8.9 %collective-permute-start.2 = (bf16[2,552,128]{2,1,0:T(8,128)(2,1)S(1)}, bf16[2,552,128]{2,1,0:T(8,128)(2,1)S(1)}, u32[]{:S(2)}, u32[]{:S(2)}) collective-permute-start(bf16[2,552,128]{2,1,0:T(8,128)(2,1)S(1)} %get-tuple-element.12), channel_id=1, source_target_pairs={{0,1},{1,2},{2,3},{3,4},{4,5},{5,6},{6,7},{7,8},{8,9},{9,10},{10,1... | collective-permute-start | bytes 847880 | tf_op jit(solution)/shard_map/ppermute | solution.py:346
  50.3 8.7 %collective-permute-start.3 = (bf16[2,552,128]{2,1,0:T(8,128)(2,1)S(1)}, bf16[2,552,128]{2,1,0:T(8,128)(2,1)S(1)}, u32[]{:S(2)}, u32[]{:S(2)}) collective-permute-start(bf16[2,552,128]{2,1,0:T(8,128)(2,1)S(1)} %get-tuple-element.13), channel_id=1, source_target_pairs={{1,0},{2,1},{3,2},{4,3},{5,4},{6,5},{7,6},{8,7},{9,8},{10,9},{11,1... | collective-permute-start | bytes 847880 | tf_op jit(solution)/shard_map/ppermute | solution.py:346
